TPU v7x, 32 devices: a whole 2x2x4 slice. The times are simulated.
32 devices in a mesh: col: 4 (over x, core), row: 8 (over z, y).
Axes of the slice: x: 2, y: 2, z: 4, core: 2. Of those that a mesh axis runs over, the one named last changes fastest.
Arguments:
- drive: float32 [8192], P(('col', 'row')), may hold values from -6 to 6
- resist: float32 [8192], P(('col', 'row')), may hold values from 1 to 4
- centers: float32 [3, 8192], P(None, 'col'), may hold values from 0 to 1
- tangents: float32 [3, 8192], P(None, 'col'), may hold values from -5 to 5
- iron_points: float32 [3, 65536], P(None, ('col', 'row')), may hold values from 0 to 1
- owner: int32 [65536, 1], P(('col', 'row')), may hold values from 0 to 7; in each aligned block of 2048 rows (0 to 2047, 2048 to 4095, ...) at most 512 rows name the same one
- range_len: int32 [8], replicated, may hold values from 256 to 1024, as said below
Outputs:
- currents: float32 [8192], P(('col', 'row'))
- iron_field: float32 [3, 65536], P(None, ('col', 'row'))
Inputs may be any that keep to these rules, and one draw needn't show every extreme that they name: `owner`: the 2048 points of one device name each block at most 512 times, and in every draw some device names some block exactly 512 times. `range_len`: some block has all 1024 segments active.
All inputs are finite; a program needn't handle non-finite values.
Results may differ from a plain program's by a relative error of at most 0.0003.
Values sent between devices are 32-bit elements; how exact they have to be, the bound alone decides.
No kernel may reach another device: no remote copies, remote signals or barrier semaphores. Data moves between devices by JAX's collectives and lax.ppermute only.
A program may use at most 64 MiB of HBM per device.

v0:
```python
import math

import jax
import jax.numpy as jnp
from jax import lax
from jax.sharding import PartitionSpec as P

KRYLOV = 2


EPS_SEG = 0.0004
EPS_FIELD = 0.0025


def tile_product(row_geo, col_geo, vector):
    diff_x = row_geo[0][:, None] - col_geo[0][None, :]
    diff_y = row_geo[1][:, None] - col_geo[1][None, :]
    diff_z = row_geo[2][:, None] - col_geo[2][None, :]
    inverse = lax.rsqrt(diff_x * diff_x + diff_y * diff_y + diff_z * diff_z + EPS_SEG)
    along = (
        row_geo[3][:, None] * col_geo[3][None, :]
        + row_geo[4][:, None] * col_geo[4][None, :]
        + row_geo[5][:, None] * col_geo[5][None, :]
    )
    return jnp.dot(along * inverse, vector, precision=lax.Precision.HIGHEST)


def block_field(points, segment, selected):
    diff_x = points[0][None, :] - segment[1][:, None]
    diff_y = points[1][None, :] - segment[2][:, None]
    diff_z = points[2][None, :] - segment[3][:, None]
    radius_sq = diff_x * diff_x + diff_y * diff_y + diff_z * diff_z + EPS_FIELD
    weight = (segment[0] * selected)[:, None] * lax.rsqrt(radius_sq) / radius_sq
    field_x = jnp.sum(
        weight * (segment[5][:, None] * diff_z - segment[6][:, None] * diff_y), axis=0
    )
    field_y = jnp.sum(
        weight * (segment[6][:, None] * diff_x - segment[4][:, None] * diff_z), axis=0
    )
    field_z = jnp.sum(
        weight * (segment[4][:, None] * diff_y - segment[5][:, None] * diff_x), axis=0
    )
    return jnp.stack([field_x, field_y, field_z])


def field_sum(points, block, mask):
    width = block.shape[1]
    part_size = math.gcd(width, 256)

    def field_accumulate(counter, total):
        segment = lax.dynamic_slice_in_dim(block, counter * part_size, part_size, 1)
        selected = lax.dynamic_slice_in_dim(mask, counter * part_size, part_size, 0)
        return total + block_field(points, segment, selected)

    empty = jnp.zeros((3, points.shape[1]), jnp.float32)
    return lax.fori_loop(0, width // part_size, field_accumulate, empty) * (1.0 / math.sqrt(width))


def shards(drive, resist, centers, tangents, iron_points, owner, range_len):
    seg_dev = drive.shape[0]
    n_col = lax.axis_size("col")
    n_row = lax.axis_size("row")
    coupling = 0.5 / math.sqrt(seg_dev * n_col * n_row)
    geometry = jnp.concatenate([centers, tangents], axis=0)
    row_index = lax.axis_index("row")
    own_geometry = lax.dynamic_slice_in_dim(geometry, row_index * seg_dev, seg_dev, 1)
    tile_rows = geometry.shape[1]
    row_part = math.gcd(tile_rows, 512)
    row_blocks = geometry.reshape(6, tile_rows // row_part, row_part).transpose(1, 0, 2)
    initial_norm = jnp.sqrt(lax.psum(jnp.sum(drive * drive), ("col", "row")))
    basis = [drive / initial_norm]
    columns = []
    for krylov_step in range(KRYLOV):
        apply_vector = basis[krylov_step]
        apply_packed = jnp.concatenate([apply_vector[None, :], own_geometry], axis=0)
        piece = lax.all_gather(apply_packed, "col", axis=1, tiled=True)
        products = lax.map(lambda row_geo: tile_product(row_geo, piece[1:], piece[0]), row_blocks)
        partial_sum = products.reshape(tile_rows)
        image = lax.psum_scatter(partial_sum, "row", scatter_dimension=0, tiled=True)
        image = resist * apply_vector + coupling * image
        coeffs = []
        rest = image
        for vector in basis:
            projected = lax.psum(jnp.sum(rest * vector), ("col", "row"))
            rest = rest - projected * vector
            coeffs.append(projected)
        length = jnp.sqrt(lax.psum(jnp.sum(rest * rest), ("col", "row")))
        columns.append((coeffs, length))
        basis.append(rest / length)
    hessen_a = columns[0][0][0]
    hessen_b = columns[0][1]
    hessen_c = columns[1][0][0]
    hessen_d = columns[1][0][1]
    hessen_e = columns[1][1]
    normal_first = hessen_a * hessen_a + hessen_b * hessen_b
    normal_cross = hessen_a * hessen_c + hessen_b * hessen_d
    normal_second = hessen_c * hessen_c + hessen_d * hessen_d + hessen_e * hessen_e
    target_first = initial_norm * hessen_a
    target_second = initial_norm * hessen_c
    determinant = normal_first * normal_second - normal_cross * normal_cross
    weight_first = (normal_second * target_first - normal_cross * target_second) / determinant
    weight_second = (normal_first * target_second - normal_cross * target_first) / determinant
    currents = weight_first * basis[0] + weight_second * basis[1]
    points_count = iron_points.shape[1]
    owners = owner[:, 0]
    packed = jnp.concatenate([currents[None, :], own_geometry], axis=0)
    block = lax.all_gather(packed, "col", axis=1, tiled=True)
    limit = lax.dynamic_index_in_dim(range_len, row_index, 0, keepdims=False)
    mask = (jnp.arange(block.shape[1]) < limit).astype(jnp.float32)
    capacity = 2 * points_count // n_row
    marks = (owners[:, None] == jnp.arange(n_row)[None, :]).astype(jnp.int32)
    ranks = jnp.sum((jnp.cumsum(marks, axis=0) - 1) * marks, axis=1)
    slots = owners * capacity + ranks
    outgoing = jnp.zeros((3, n_row * capacity), jnp.float32).at[:, slots].set(iron_points)
    outgoing = outgoing.reshape(3, n_row, capacity)
    received = lax.all_to_all(outgoing, "row", split_axis=1, concat_axis=1, tiled=True)
    returned = field_sum(received.reshape(3, -1), block, mask).reshape(received.shape)
    back = lax.all_to_all(returned, "row", split_axis=1, concat_axis=1, tiled=True)
    iron_field = back.reshape(3, n_row * capacity)[:, slots]
    return (currents, iron_field)


def solution(mesh):
    return jax.shard_map(
        shards,
        mesh=mesh,
        in_specs=(
            P(("col", "row")),
            P(("col", "row")),
            P(None, "col"),
            P(None, "col"),
            P(None, ("col", "row")),
            P(("col", "row"), None),
            P(),
        ),
        out_specs=(P(("col", "row")), P(None, ("col", "row"))),
        check_vma=False,
    )
```

profile of v0, /device:TPU:0, one launch (start us, length us, event | category | flops | bytes accessed | tf_op | source)
XLA Modules:
  0.0 400.5 jit_solution(313155150767368609)
XLA Ops:
  6.8 6.1 %scatter_custom_fusion = f32[3,4096]{0,1:T(8,128)S(1)} fusion(s32[2048]{0:T(1024)S(1)} %bitcast.202, f32[2048,3]{1,0:T(8,128)S(1)} %copy.25, f32[]{:T(128)} %constant.84.clone.1), kind=kCustom, calls=%fused_computation.105 | custom fusion | bytes 49156 | tf_op jit(solution)/shard_map/scatter | solution.py:114
  14.1 7.3 %all-to-all-start = ((f32[3,8,512]{2,0,1:T(4,128)}), f32[3,8,512]{2,0,1:T(4,128)S(1)}, u32[]{:S(2)}, u32[]{:S(2)}) async-start(f32[3,8,512]{2,0,1:T(4,128)} %copy.26), calls=%async_computation | async-start | bytes 131072 | tf_op jit(solution)/shard_map/all_to_all | solution.py:116
  22.1 41.0 %psum.42 = f32[]{:T(128)} all-reduce(f32[]{:T(128)} %multiply_reduce_fusion.5), channel_id=1, replica_groups=mesh['col'=4,'row'=8] {'col','row'}, use_global_device_ids=true, to_apply=%region_1.0 | all-reduce | flops 1 | bytes 8 | tf_op jit(solution)/shard_map/psum | solution.py:70
  63.8 5.5 %all_gather.9 = f32[7,1024]{1,0:T(8,128)S(1)} all-gather(f32[7,256]{1,0:T(8,128)S(1)} %pad_maximum_fusion.1), channel_id=1, replica_groups=mesh['col'=4,'row'=8] {'col'}, dimensions={1}, use_global_device_ids=true | all-gather | bytes 35840 | tf_op jit(solution)/shard_map/all_gather | solution.py:76
  69.3 12.7 %while.34 = (s32[]{:T(128)}, f32[4,512]{1,0:T(4,128)S(1)}, f32[4,6,512]{2,1,0:T(8,128)S(1)}, f32[7,1024]{1,0:T(8,128)S(1)}, s32[]{:T(128)}, /*index=5*/s32[]{:T(128)}, s32[]{}, s32[]{}, s32[]{}, s32[]{}, /*index=10*/s32[]{}) while((s32[]{:T(128)}, f32[4,512]{1,0:T(4,128)S(1)}, f32[4,6,512]{2,1,0:T(8,128)S(1)}, f32[7,1024]{1,0:T(8,128)S(1)}, ...), condition=%wide.region_3.4_spmd, body=%wide.region_2.3_spmd.sunk | while | flops 14155783 | bytes 121029 | solution.py:77
  82.1 21.2 %all-reduce = f32[2048]{0:T(1024)S(1)} all-reduce(f32[2048]{0:T(1024)S(1)} %bitcast.206), channel_id=2, replica_groups=mesh['col'=4,'row'=8] {'row'}, use_global_device_ids=true, to_apply=%region_4.5.clone | all-reduce | flops 2048 | bytes 16384
  105.3 37.1 %psum.43 = f32[]{:T(128)} all-reduce(f32[]{:T(128)} %multiply_reduce_fusion.4), channel_id=1, replica_groups=mesh['col'=4,'row'=8] {'col','row'}, use_global_device_ids=true, to_apply=%region_6.7 | all-reduce | flops 1 | bytes 8 | tf_op jit(solution)/shard_map/psum | solution.py:84
  143.6 41.8 %psum.44 = f32[]{:T(128)} all-reduce(f32[]{:T(128)} %get-tuple-element.200), channel_id=1, replica_groups=mesh['col'=4,'row'=8] {'col','row'}, use_global_device_ids=true, to_apply=%region_8.9 | all-reduce | flops 1 | bytes 8 | tf_op jit(solution)/shard_map/psum | solution.py:87
  186.1 5.5 %all_gather.10 = f32[7,1024]{1,0:T(8,128)S(1)} all-gather(f32[7,256]{1,0:T(8,128)S(1)} %pad_maximum_fusion.2), channel_id=1, replica_groups=mesh['col'=4,'row'=8] {'col'}, dimensions={1}, use_global_device_ids=true | all-gather | bytes 35840 | tf_op jit(solution)/shard_map/all_gather | solution.py:76
  191.7 12.7 %while.35 = (s32[]{:T(128)}, f32[4,512]{1,0:T(4,128)S(1)}, f32[4,6,512]{2,1,0:T(8,128)S(1)}, f32[7,1024]{1,0:T(8,128)S(1)}, s32[]{:T(128)}, /*index=5*/s32[]{:T(128)}, s32[]{}, s32[]{}, s32[]{}, s32[]{}, /*index=10*/s32[]{}) while((s32[]{:T(128)}, f32[4,512]{1,0:T(4,128)S(1)}, f32[4,6,512]{2,1,0:T(8,128)S(1)}, f32[7,1024]{1,0:T(8,128)S(1)}, ...), condition=%wide.region_10.11_spmd, body=%wide.region_9.10_spmd.sunk | while | flops 14155783 | bytes 121029 | solution.py:77
  191.7 3.1 fusion.110
  204.4 20.5 %all-reduce.1 = f32[2048]{0:T(1024)S(1)} all-reduce(f32[2048]{0:T(1024)S(1)} %bitcast.207), channel_id=3, replica_groups=mesh['col'=4,'row'=8] {'row'}, use_global_device_ids=true, to_apply=%region_11.12.clone | all-reduce | flops 2048 | bytes 16384
  225.6 37.2 %psum.45 = f32[]{:T(128)} all-reduce(f32[]{:T(128)} %get-tuple-element.198), channel_id=1, replica_groups=mesh['col'=4,'row'=8] {'col','row'}, use_global_device_ids=true, to_apply=%region_13.14 | all-reduce | flops 1 | bytes 8 | tf_op jit(solution)/shard_map/psum | solution.py:84
  266.1 42.7 %psum.46 = f32[]{:T(128)} all-reduce(f32[]{:T(128)} %multiply_reduce_fusion.1), channel_id=1, replica_groups=mesh['col'=4,'row'=8] {'col','row'}, use_global_device_ids=true, to_apply=%region_15.16 | all-reduce | flops 1 | bytes 8 | tf_op jit(solution)/shard_map/psum | solution.py:84
  315.8 38.9 %psum.47 = f32[]{:T(128)} all-reduce(f32[]{:T(128)} %multiply_reduce_fusion), channel_id=1, replica_groups=mesh['col'=4,'row'=8] {'col','row'}, use_global_device_ids=true, to_apply=%region_17.18 | all-reduce | flops 1 | bytes 8 | tf_op jit(solution)/shard_map/psum | solution.py:87
  355.5 5.5 %all_gather.11 = f32[7,1024]{1,0:T(8,128)S(1)} all-gather(f32[7,256]{1,0:T(8,128)S(1)} %pad_maximum_fusion.3), channel_id=1, replica_groups=mesh['col'=4,'row'=8] {'col'}, dimensions={1}, use_global_device_ids=true | all-gather | bytes 35840 | tf_op jit(solution)/shard_map/all_gather | solution.py:107
  362.3 18.5 %while.36 = (s32[]{:T(128)}, f32[3,4096]{1,0:T(4,128)S(1)}, f32[7,1024]{1,0:T(8,128)S(1)}, f32[1024]{0:T(1024)S(1)}, f32[3,4096]{1,0:T(4,128)S(1)}, /*index=5*/s...) while((s32[]{:T(128)}, f32[3,4096]{1,0:T(4,128)S(1)}, ...), condition=%wide.region_26.27_spmd.clone, body=%wide.region_22.26_spmd.clone.sunk | while | flops 27300108 | bytes 368941 | solution.py:56
  362.5 4.3 %fusion.113 = (f32[4096]{0:T(1024)S(1)}, f32[4096]{0:T(1024)S(1)}, f32[4096]{0:T(1024)S(1)}) fusion(f32[256]{0:T(256)S(1)} %bitcast.209, f32[256]{0:T(256)S(1)} %bitcast.210, f32[256]{0:T(256)S(1)} %bitcast.211, f32[4096]{0:T(1024)S(1)} %bitcast.168, f32[256]{0:T(256)S(1)} %bitcast.212, f32[4096]{0:T(1024)S(1)} %bitcast.169, f32[256]{0:T(256)S(1)} %bitcast.213, ...), kind=kLoop, calls=%fused_computation.100.clone.1 | loop fusion | flops 27250688 | bytes 105472 | tf_op jit(solution)/shard_map/while/body/eval_jaxpr/reduce_sum | solution.py:34
  367.2 4.3 %fusion.113 = (f32[4096]{0:T(1024)S(1)}, f32[4096]{0:T(1024)S(1)}, f32[4096]{0:T(1024)S(1)}) fusion(f32[256]{0:T(256)S(1)} %bitcast.209, f32[256]{0:T(256)S(1)} %bitcast.210, f32[256]{0:T(256)S(1)} %bitcast.211, f32[4096]{0:T(1024)S(1)} %bitcast.168, f32[256]{0:T(256)S(1)} %bitcast.212, f32[4096]{0:T(1024)S(1)} %bitcast.169, f32[256]{0:T(256)S(1)} %bitcast.213, ...), kind=kLoop, calls=%fused_computation.100.clone.1 | loop fusion | flops 27250688 | bytes 105472 | tf_op jit(solution)/shard_map/while/body/eval_jaxpr/reduce_sum | solution.py:34
  371.8 4.3 %fusion.113 = (f32[4096]{0:T(1024)S(1)}, f32[4096]{0:T(1024)S(1)}, f32[4096]{0:T(1024)S(1)}) fusion(f32[256]{0:T(256)S(1)} %bitcast.209, f32[256]{0:T(256)S(1)} %bitcast.210, f32[256]{0:T(256)S(1)} %bitcast.211, f32[4096]{0:T(1024)S(1)} %bitcast.168, f32[256]{0:T(256)S(1)} %bitcast.212, f32[4096]{0:T(1024)S(1)} %bitcast.169, f32[256]{0:T(256)S(1)} %bitcast.213, ...), kind=kLoop, calls=%fused_computation.100.clone.1 | loop fusion | flops 27250688 | bytes 105472 | tf_op jit(solution)/shard_map/while/body/eval_jaxpr/reduce_sum | solution.py:34
  376.4 4.3 %fusion.113 = (f32[4096]{0:T(1024)S(1)}, f32[4096]{0:T(1024)S(1)}, f32[4096]{0:T(1024)S(1)}) fusion(f32[256]{0:T(256)S(1)} %bitcast.209, f32[256]{0:T(256)S(1)} %bitcast.210, f32[256]{0:T(256)S(1)} %bitcast.211, f32[4096]{0:T(1024)S(1)} %bitcast.168, f32[256]{0:T(256)S(1)} %bitcast.212, f32[4096]{0:T(1024)S(1)} %bitcast.169, f32[256]{0:T(256)S(1)} %bitcast.213, ...), kind=kLoop, calls=%fused_computation.100.clone.1 | loop fusion | flops 27250688 | bytes 105472 | tf_op jit(solution)/shard_map/while/body/eval_jaxpr/reduce_sum | solution.py:34
  381.5 5.1 %all-to-all-start.1 = ((f32[3,8,512]{2,0,1:T(4,128)}), f32[3,8,512]{2,0,1:T(4,128)S(1)}, u32[]{:S(2)}, u32[]{:S(2)}) async-start(f32[3,8,512]{2,0,1:T(4,128)} %bitcast.45), calls=%async_computation.1 | async-start | bytes 131072 | tf_op jit(solution)/shard_map/all_to_all | solution.py:118
  386.5 6.9 %all-to-all-done.1 = f32[3,8,512]{2,0,1:T(4,128)S(1)} async-done(((f32[3,8,512]{2,0,1:T(4,128)}), f32[3,8,512]{2,0,1:T(4,128)S(1)}, u32[]{:S(2)}, u32[]{:S(2)}) %all-to-all-start.1) | async-done | bytes 49184 | tf_op jit(solution)/shard_map/all_to_all | solution.py:118
  394.1 5.5 %gather_fusion = f32[2048,3]{1,0:T(8,128)S(1)} fusion(f32[3,4096]{0,1:T(8,128)S(1)} %bitcast.163, s32[2048]{0:T(1024)S(1)} %broadcast_clamp_fusion), kind=kCustom, calls=%fused_computation | custom fusion | bytes 57344 | tf_op jit(solution)/shard_map/gather | solution.py:119
  (97 shorter events, 41.3 us)
Async XLA Ops:
  6.7 14.7 %copy-start = (f32[3,2048]{1,0:T(4,128)S(1)}, f32[3,2048]{1,0:T(4,128)}, u32[]{:S(2)}) copy-start(f32[3,2048]{1,0:T(4,128)} %param.16) | copy-start | bytes 73732
  6.8 14.7 %copy-start.1 = (f32[3,2048]{1,0:T(4,128)S(1)}, f32[3,2048]{1,0:T(4,128)}, u32[]{:S(2)}) copy-start(f32[3,2048]{1,0:T(4,128)} %param.15) | copy-start | bytes 73732
  6.8 14.8 %copy-start.2 = (f32[256]{0:T(256)S(1)}, f32[256]{0:T(256)}, u32[]{:S(2)}) copy-start(f32[256]{0:T(256)} %param.13) | copy-start | bytes 3076
  14.1 348.2 %all-to-all-start = ((f32[3,8,512]{2,0,1:T(4,128)}), f32[3,8,512]{2,0,1:T(4,128)S(1)}, u32[]{:S(2)}, u32[]{:S(2)}) async-start(f32[3,8,512]{2,0,1:T(4,128)} %copy.26), calls=%async_computation | async-start | bytes 131072 | tf_op jit(solution)/shard_map/all_to_all | solution.py:116
  69.3 34.0 %copy-start.6 = (u32[32]{0:T(128)S(1)}, u32[32]{0:T(128)}, u32[]{:S(2)}) copy-start(u32[32]{0:T(128)} %constant.97) | copy-start | bytes 388
  69.3 35.2 %copy-start.3 = (f32[256]{0:T(256)S(1)}, f32[256]{0:T(256)}, u32[]{:S(2)}) copy-start(f32[256]{0:T(256)} %param.14) | copy-start | bytes 3076
  191.7 169.4 %copy-start.5 = (s32[8]{0:T(128)S(1)}, s32[8]{0:T(128)}, u32[]{:S(2)}) copy-start(s32[8]{0:T(128)} %param.19) | copy-start | bytes 100
  355.5 6.8 %copy-start.4 = (f32[256]{0:T(256)}, f32[256]{0:T(256)S(1)}, u32[]{:S(2)}) copy-start(f32[256]{0:T(256)S(1)} %multiply_add_fusion) | copy-start | bytes 3076
  381.5 12.0 %all-to-all-start.1 = ((f32[3,8,512]{2,0,1:T(4,128)}), f32[3,8,512]{2,0,1:T(4,128)S(1)}, u32[]{:S(2)}, u32[]{:S(2)}) async-start(f32[3,8,512]{2,0,1:T(4,128)} %bitcast.45), calls=%async_computation.1 | async-start | bytes 131072 | tf_op jit(solution)/shard_map/all_to_all | solution.py:118
where the time goes:
time: 402 us; the launch traced here: 400 us
  blocking collectives  297 us (74%)
  other arithmetic  30.4 us (8%)
  matrix products  24.5 us (6%)
  local copies, waits for them, and re-layouts  18.3 us (5%)
  starting transfers between devices  12.4 us (3%)
  between operations  10.8 us (3%)
  waiting for transfers between devices  6.9 us (2%)
    psum x3, blocking collectives, shards(): projected = lax.psum(jnp.sum(rest * vector), ('col', 'row'))  117 us
    psum x2, blocking collectives, shards(): length = jnp.sqrt(lax.psum(jnp.sum(rest * rest), ('col', 'row')))  80.7 us
    unnamed x2, blocking collectives  41.8 us
    psum x1, blocking collectives, shards(): initial_norm = jnp.sqrt(lax.psum(jnp.sum(drive * drive), ('col', 'row')))  41 us
    dot_general x8, matrix products, tile_product(): return jnp.dot(along * inverse, vector, precision=lax.Precision.HIGHEST)  24.5 us
    reduce_sum x4, other arithmetic, block_field(): jnp.sum(weight * (segment[5][:, None] * diff_z - segment[6][:, None] * di...  17.2 us
    all_gather x2, blocking collectives, shards(): piece = lax.all_gather(apply_packed, 'col', axis=1, tiled=True)  11 us
  transfers between devices with their start and end apart: 2, of which 1 were waited for; matrix products, arithmetic and copies ran while one was open for 8% of the time, Pallas kernels for 0%

commit v1 on v0

v1 whole, which is shorter than its diff:
```python
import functools
import math

import jax
import jax.numpy as jnp
from jax import lax
from jax.experimental import pallas as pl
from jax.experimental.pallas import tpu as pltpu
from jax.sharding import PartitionSpec as P

EPS_SEG = 0.0004
EPS_FIELD = 0.0025
AXES = ("col", "row")
CHUNK = 128
VMEM_LIMIT = 48 * 1024 * 1024


def split3(x):
    high = x.astype(jnp.bfloat16).astype(jnp.float32)
    rest = x - high
    middle = rest.astype(jnp.bfloat16).astype(jnp.float32)
    low = (rest - middle).astype(jnp.bfloat16).astype(jnp.float32)
    return high, middle, low


def left_parts(x):
    high, middle, low = split3(x)
    return jnp.concatenate([high, high, middle, middle, high, low], axis=0).astype(jnp.bfloat16)


def right_parts(x):
    high, middle, low = split3(x)
    return jnp.concatenate([high, middle, high, middle, low, high], axis=0).astype(jnp.bfloat16)


def rows8(*rows):
    width = rows[0].shape[1]
    count = sum(r.shape[0] for r in rows)
    if count < 8:
        rows = rows + (jnp.zeros((8 - count, width), jnp.float32),)
    return jnp.concatenate(rows, axis=0)


def moving_center(c):
    square = jnp.sum(c * c, axis=0, keepdims=True)
    return rows8(-2.0 * c, jnp.ones_like(square), square)


def fixed_center(c, eps):
    square = jnp.sum(c * c, axis=0, keepdims=True) + eps
    return rows8(c, square, jnp.ones_like(square))


def dot(a, b):
    return jnp.dot(a, b, preferred_element_type=jnp.float32)


def dot_nt(a, b):
    return lax.dot_general(a, b, (((1,), (1,)), ((), ())), preferred_element_type=jnp.float32)


def couple(own_ref, geo_ref, vec_ref, acc_ref, tile):
    own = own_ref[...]
    count = geo_ref.shape[1] // tile
    lc = transposed(left_parts_f32(moving_center(own[0:3] - 0.5)))
    lt = transposed(left_parts_f32(rows8(own[3:6])))
    acc_ref[...] = jnp.zeros_like(acc_ref)

    def step(k, carry):
        at = pl.ds(pl.multiple_of(k * tile, tile), tile)
        geo = geo_ref[:, at]
        vec = vec_ref[:, at]
        rc = right_parts(fixed_center(geo[0:3] - 0.5, EPS_SEG))
        rt = right_parts(rows8(geo[3:6] * vec))
        pair = dot(lt, rt) * lax.rsqrt(dot(lc, rc))
        total = pair[:, 0:128]
        for piece in range(1, tile // 128):
            total = total + pair[:, piece * 128:(piece + 1) * 128]
        acc_ref[...] += total
        return carry

    lax.fori_loop(0, count, step, 0)
    return jnp.sum(acc_ref[...].T, axis=0, keepdims=True)


def left_parts_f32(x):
    high, middle, low = split3(x)
    return jnp.concatenate([high, high, middle, middle, high, low], axis=0)


def transposed(x):
    return x.T.astype(jnp.bfloat16)


def first_kernel(coupling, own_ref, geo_ref, drive_ref, drive_own_ref, resist_ref, image_ref, vec_ref, acc_ref, *, tile):
    drive = drive_ref[...]
    scale = 1.0 / jnp.sqrt(jnp.sum(drive * drive, keepdims=True))
    vec_ref[...] = drive * scale
    product = couple(own_ref, geo_ref, vec_ref, acc_ref, tile)
    image_ref[...] = resist_ref[...] * (drive_own_ref[...] * scale) + coupling * product


def second_kernel(
    coupling, own_ref, geo_ref, drive_ref, image_ref, drive_own_ref, image_own_ref, resist_ref,
    basis_ref, basis_own_ref, stats_ref, vec_ref, acc_ref, *, tile
):
    drive = drive_ref[...]
    norm_sq = jnp.sum(drive * drive, keepdims=True)
    norm = jnp.sqrt(norm_sq)
    scale = 1.0 / norm
    basis_a = drive * scale
    image = image_ref[...]
    hessen_a = jnp.sum(image * basis_a, keepdims=True)
    rest = image - hessen_a * basis_a
    hessen_b = jnp.sqrt(jnp.sum(rest * rest, keepdims=True))
    inverse = 1.0 / hessen_b
    basis_b = rest * inverse
    vec_ref[...] = basis_b
    basis_ref[0:1, :] = basis_a
    basis_ref[1:2, :] = basis_b
    own_a = drive_own_ref[...] * scale
    own_b = (image_own_ref[...] - hessen_a * own_a) * inverse
    basis_own_ref[0:1, :] = own_a
    basis_own_ref[1:2, :] = own_b
    product = couple(own_ref, geo_ref, vec_ref, acc_ref, tile)
    second = resist_ref[...] * own_b + coupling * product
    lane = lax.broadcasted_iota(jnp.int32, (1, 128), 1)
    part_c = jnp.sum(second * own_a, keepdims=True)
    part_d = jnp.sum(second * own_b, keepdims=True)
    part_s = jnp.sum(second * second, keepdims=True)
    stats_ref[0:1, :] = jnp.where(lane == 0, part_c, jnp.where(lane == 1, part_d, jnp.where(lane == 2, part_s, 0.0)))
    stats_ref[1:2, :] = jnp.where(lane == 0, norm, jnp.where(lane == 1, hessen_a, jnp.where(lane == 2, hessen_b, 0.0)))


def field_kernel(counts_ref, length_ref, points_ref, geo_ref, basis_ref, out_ref, rc_ref, table_ref, *, n_col, n_row, seg_dev, capacity):
    width = n_col * seg_dev
    quarter = width // 4
    scale = 1.0 / math.sqrt(width)
    lane = lax.broadcasted_iota(jnp.int32, (1, seg_dev), 1)

    def block_step(block, carry):
        length = length_ref[block]
        for col in range(n_col):
            at = pl.ds(pl.multiple_of((col * n_row + block) * seg_dev, seg_dev), seg_dev)
            to = pl.ds(col * seg_dev, seg_dev)
            geo = geo_ref[:, at]
            center = geo[0:3] - 0.5
            tangent = geo[3:6]
            rc_ref[:, to] = right_parts(fixed_center(center, EPS_FIELD))
            cross = jnp.concatenate([
                tangent[1:2] * center[2:3] - tangent[2:3] * center[1:2],
                tangent[2:3] * center[0:1] - tangent[0:1] * center[2:3],
                tangent[0:1] * center[1:2] - tangent[1:2] * center[0:1],
            ], axis=0)
            both = rows8(tangent, cross)
            active = jnp.where(lane + col * seg_dev < length, scale, 0.0)
            first = both * (basis_ref[0:1, at] * active)
            second = both * (basis_ref[1:2, at] * active)
            parts = jnp.concatenate([first, second], axis=0)
            high = parts.astype(jnp.bfloat16).astype(jnp.float32)
            table_ref[:, to] = jnp.concatenate([high, parts - high], axis=0).astype(jnp.bfloat16)
        chunks = (counts_ref[block] + CHUNK - 1) // CHUNK
        tiles = (length + quarter - 1) // quarter

        def chunk_step(chunk, carry):
            at = pl.ds(pl.multiple_of(block * capacity + chunk * CHUNK, CHUNK), CHUNK)
            left = transposed(left_parts_f32(moving_center(points_ref[:, at] - 0.5)))
            for size in range(1, 5):
                @pl.when(tiles == size)
                def _():
                    used = size * quarter
                    inverse = lax.rsqrt(dot(left, rc_ref[:, 0:used]))
                    cube = inverse * inverse * inverse
                    high = cube.astype(jnp.bfloat16)
                    low = (cube - high.astype(jnp.float32)).astype(jnp.bfloat16)
                    table = table_ref[:, 0:used]
                    total = dot_nt(high, table) + dot_nt(low, table)
                    total = total.T
                    out_ref[:, at] = total[0:16] + total[16:32]
            return carry

        lax.fori_loop(0, chunks, chunk_step, 0)
        return carry

    lax.fori_loop(0, n_row, block_step, 0)


def shift_sum(x, axis):
    size = lax.axis_size(axis)
    total = x
    for shift in range(1, size):
        total = total + lax.ppermute(x, axis, [(i, (i + shift) % size) for i in range(size)])
    return total


def shards(drive, resist, centers, tangents, iron_points, owner, range_len):
    seg_dev = drive.shape[0]
    n_col = lax.axis_size("col")
    n_row = lax.axis_size("row")
    n_dev = n_col * n_row
    segments = seg_dev * n_dev
    coupling = 0.5 / math.sqrt(segments)
    geometry = jnp.concatenate([centers, tangents], axis=0)
    row_index = lax.axis_index("row")
    own = lax.dynamic_slice_in_dim(geometry, row_index * seg_dev, seg_dev, 1)
    params = pltpu.CompilerParams(vmem_limit_bytes=VMEM_LIMIT)
    tile = 512
    drive_own = drive[None, :]
    resist_own = resist[None, :]
    drive_all = lax.all_gather(drive, AXES, axis=0, tiled=True)[None, :]
    geo_all = lax.all_gather(geometry, "col", axis=1, tiled=True)
    scratch = [pltpu.VMEM((1, segments), jnp.float32), pltpu.VMEM((seg_dev, 128), jnp.float32)]
    image_own = pl.pallas_call(
        functools.partial(first_kernel, coupling, tile=tile),
        out_shape=jax.ShapeDtypeStruct((1, seg_dev), jnp.float32),
        scratch_shapes=scratch,
        compiler_params=params,
        name="first_image",
    )(own, geo_all, drive_all, drive_own, resist_own)
    spread = jnp.broadcast_to(image_own, (n_dev, seg_dev))
    image_all = lax.all_to_all(spread, AXES, 0, 0, tiled=True).reshape(1, segments)
    basis, basis_own, stats = pl.pallas_call(
        functools.partial(second_kernel, coupling, tile=tile),
        out_shape=(
            jax.ShapeDtypeStruct((2, segments), jnp.float32),
            jax.ShapeDtypeStruct((2, seg_dev), jnp.float32),
            jax.ShapeDtypeStruct((2, 128), jnp.float32),
        ),
        scratch_shapes=scratch,
        compiler_params=params,
        name="second_image",
    )(own, geo_all, drive_all, image_all, drive_own, image_own, resist_own)
    sums = shift_sum(shift_sum(stats[0:1], "col"), "row")

    points_count = iron_points.shape[1]
    owners = owner[:, 0]
    capacity = 2 * points_count // n_row
    marks = (owners[:, None] == jnp.arange(n_row)[None, :]).astype(jnp.int32)
    ranks = jnp.sum((jnp.cumsum(marks, axis=0) - 1) * marks, axis=1)
    counts = jnp.sum(marks, axis=0)
    slots = owners * capacity + ranks
    grouped = jnp.zeros((3, n_row * capacity), jnp.float32).at[:, slots].set(iron_points)
    smem = pl.BlockSpec(memory_space=pltpu.SMEM)
    vmem = pl.BlockSpec(memory_space=pltpu.VMEM)
    field = pl.pallas_call(
        functools.partial(field_kernel, n_col=n_col, n_row=n_row, seg_dev=seg_dev, capacity=capacity),
        out_shape=jax.ShapeDtypeStruct((16, n_row * capacity), jnp.float32),
        in_specs=[smem, smem, vmem, vmem, vmem],
        scratch_shapes=[
            pltpu.VMEM((48, n_col * seg_dev), jnp.bfloat16),
            pltpu.VMEM((32, n_col * seg_dev), jnp.bfloat16),
        ],
        compiler_params=params,
        name="block_field",
    )(counts, range_len, grouped, geo_all, basis)

    initial_norm = stats[1, 0]
    hessen_a = stats[1, 1]
    hessen_b = stats[1, 2]
    hessen_c = sums[0, 0]
    hessen_d = sums[0, 1]
    normal_first = hessen_a * hessen_a + hessen_b * hessen_b
    normal_cross = hessen_a * hessen_c + hessen_b * hessen_d
    normal_second = sums[0, 2]
    target_first = initial_norm * hessen_a
    target_second = initial_norm * hessen_c
    determinant = normal_first * normal_second - normal_cross * normal_cross
    weight_first = (normal_second * target_first - normal_cross * target_second) / determinant
    weight_second = (normal_first * target_second - normal_cross * target_first) / determinant
    currents = weight_first * basis_own[0] + weight_second * basis_own[1]
    moments = (weight_first * field[0:6] + weight_second * field[8:14])[:, slots]
    px, py, pz = iron_points[0] - 0.5, iron_points[1] - 0.5, iron_points[2] - 0.5
    iron_field = jnp.stack([
        pz * moments[1] - py * moments[2] - moments[3],
        px * moments[2] - pz * moments[0] - moments[4],
        py * moments[0] - px * moments[1] - moments[5],
    ])
    return (currents, iron_field)


def solution(mesh):
    return jax.shard_map(
        shards,
        mesh=mesh,
        in_specs=(
            P(AXES),
            P(AXES),
            P(None, "col"),
            P(None, "col"),
            P(None, AXES),
            P(AXES, None),
            P(),
        ),
        out_specs=(P(AXES), P(None, AXES)),
        check_vma=False,
    )
```

time: 402 us -> 154 us (0.38)
  blocking collectives: 297 us -> 76.2 us
  matrix products: 24.5 us -> 0 us
  Pallas kernels: 0 us -> 22.9 us
  other arithmetic: 30.4 us -> 8.96 us
  waiting for transfers between devices: 6.9 us -> 2.12 us
    psum x6 -> x0, blocking collectives: 239 us -> none  [the longest x3 117 us: shards(): projected = lax.psum(jnp.sum(rest * vector), ('col', 'row'))]
    all_gather x3 -> x2, blocking collectives: 16.5 us -> 76.2 us  [the longest x1 69.1 us: shards(): drive_all = lax.all_gather(drive, AXES, axis=0, tiled=True)[None, :]]
    unnamed x2 -> x0, blocking collectives: 41.8 us -> none
    dot_general x8 -> x0, matrix products: 24.5 us -> none  [tile_product(): return jnp.dot(along * inverse, vector, precision=lax.Precision.HIGHEST)]
    reduce_sum x10 -> x0, other arithmetic: 23.6 us -> none  [the longest x4 17.2 us: block_field(): jnp.sum(weight * (segment[5][:, None] * diff_z - segment[6][:, None] * di...]
    pallas_call x0 -> x3, Pallas kernels: none -> 22.9 us  [the longest x1 12.3 us: shards(): pl.pallas_call(functools.partial(field_kernel, n_col=n_col, n_row=n_row,...]
    ppermute x0 -> x10, starting transfers between devices: none -> 10.8 us  [shift_sum(): lax.ppermute(x, axis, [(i, (i + shift) % size) for i in range(size)])]
    all_to_all x2 -> x1, starting transfers between devices: 12.4 us -> 2.57 us  [shards(): lax.all_to_all(spread, AXES, 0, 0, tiled=True).reshape(1, segments)]
  transfers between devices with their start and end apart: 2 -> 11, of which waited for: 1 -> 1; matrix products, arithmetic and copies ran while one was open for 8% -> 9% of each run, Pallas kernels for 0% -> 8%
where the time goes in v1:
time: 154 us; the launch traced here: 153 us
  blocking collectives  76.2 us (49%)
  Pallas kernels  22.9 us (15%)
  local copies, waits for them, and re-layouts  19.7 us (13%)
  starting transfers between devices  13.4 us (9%)
  between operations  9.73 us (6%)
  other arithmetic  8.96 us (6%)
  waiting for transfers between devices  2.12 us (1%)
    all_gather x1, blocking collectives, shards(): drive_all = lax.all_gather(drive, AXES, axis=0, tiled=True)[None, :]  69.1 us
    pallas_call x1, Pallas kernels, shards(): pl.pallas_call(functools.partial(field_kernel, n_col=n_col, n_row=n_row,...  12.3 us
    ppermute x10, starting transfers between devices, shift_sum(): lax.ppermute(x, axis, [(i, (i + shift) % size) for i in range(size)])  10.8 us
    all_gather x1, blocking collectives, shards(): geo_all = lax.all_gather(geometry, 'col', axis=1, tiled=True)  7.18 us
    scatter x2, local copies, waits for them, and re-layouts, shards(): jnp.zeros((3, n_row * capacity), jnp.float32).at[:, slots].set(iron_points)  6.72 us
    gather x2, local copies, waits for them, and re-layouts, shards(): (weight_first * field[0:6] + weight_second * field[8:14])[:, slots]  5.79 us
    pallas_call x1, Pallas kernels, shards(): pl.pallas_call(functools.partial(second_kernel, coupling, tile=tile), out...  5.55 us
    pallas_call x1, Pallas kernels, shards(): pl.pallas_call(functools.partial(first_kernel, coupling, tile=tile), out_...  5.04 us
  transfers between devices with their start and end apart: 11, of which 1 were waited for; matrix products, arithmetic and copies ran while one was open for 9% of the time, Pallas kernels for 8%

profile of v1, /device:TPU:0, one launch (start us, length us, event | category | flops | bytes accessed | tf_op | source)
XLA Modules:
  0.0 153.1 jit_solution(9035233882957210403)
XLA Ops:
  0.6 0.8 pad_maximum_fusion
  1.4 0.8 fusion.6.own_ref
  2.2 7.2 %all_gather.6.geo_ref = f32[6,8192]{1,0:T(8,128)S(1)} all-gather(f32[6,2048]{1,0:T(8,128)S(1)} %pad_maximum_fusion), channel_id=1, replica_groups=mesh['col'=4,'row'=8] {'col'}, dimensions={1}, use_global_device_ids=true | all-gather | bytes 245760 | tf_op jit(solution)/shard_map/all_gather | solution.py:211
  9.4 69.1 %all-gather = f32[32,1,256]{2,1,0:T(1,128)S(1)} all-gather(f32[1,1,256]{2,1,0:T(1,128)} %bitcast.33), channel_id=1, replica_groups=mesh['col'=4,'row'=8] {'col','row'}, dimensions={0}, use_global_device_ids=true | all-gather | bytes 33792 | tf_op jit(solution)/shard_map/all_gather | solution.py:210
  78.5 0.7 copy-done
  79.1 0.7 copy-done.2
  79.8 5.0 %first_image.1.image_own_ref = f32[1,256]{1,0:T(1,128)S(1)} custom-call(f32[6,256]{1,0:T(8,128)S(1)} %fusion.6.own_ref, f32[6,8192]{1,0:T(8,128)S(1)} %all_gather.6.geo_ref, f32[1,8192]{1,0:T(1,128)S(1)} %bitcast.30, f32[1,256]{1,0:T(1,128)S(1)} %bitcast.34, f32[1,256]{1,0:T(1,128)S(1)} %bitcast.37), custom_call_target="tpu_custom_call" | custom-call | tf_op jit(solution)/shard_map/first_image/pallas_call | solution.py:213
  85.5 2.6 %all-to-all-start = ((f32[32,1,256]{2,1,0:T(1,128)}), f32[32,1,256]{2,1,0:T(1,128)S(1)}, u32[]{:S(2)}, u32[]{:S(2)}) async-start(f32[32,1,256]{2,1,0:T(1,128)} %broadcast_in_dim.23), calls=%async_computation | async-start | bytes 65536 | tf_op jit(solution)/shard_map/all_to_all | solution.py:221
  88.1 0.7 fusion.5
  88.8 2.3 %reduce-window.6 = s32[8,16,128]{2,1,0:T(8,128)S(1)} reduce-window(s32[8,16,128]{2,1,0:T(8,128)S(1)} %fusion.5, s32[]{:T(128)} %constant.9.clone.1), window={size=1x1x128 pad=0_0x0_0x127_0}, to_apply=%region_1.2 | reduce-window | flops 2080768 | bytes 131076 | tf_op jit(solution)/shard_map/reduce-window
  91.6 0.9 fusion.4
  92.5 0.7 compare_select_fusion
  93.2 2.1 %all-to-all-done = f32[32,1,256]{2,1,0:T(1,128)S(1)} async-done(((f32[32,1,256]{2,1,0:T(1,128)}), f32[32,1,256]{2,1,0:T(1,128)S(1)}, u32[]{:S(2)}, u32[]{:S(2)}) %all-to-all-start) | async-done | bytes 32800 | tf_op jit(solution)/shard_map/all_to_all | solution.py:221
  95.3 0.7 copy-done.1
  96.6 5.6 %second_image.1 = (f32[2,8192]{1,0:T(2,128)S(1)}, f32[2,256]{1,0:T(2,128)S(1)}, f32[2,128]{1,0:T(2,128)S(1)}) custom-call(f32[6,256]{1,0:T(8,128)S(1)} %fusion.6.own_ref, f32[6,8192]{1,0:T(8,128)S(1)} %all_gather.6.geo_ref, f32[1,8192]{1,0:T(1,128)S(1)} %bitcast.31, f32[1,8192]{1,0:T(1,128)S(1)} %bitcast.32, f32[1,256]{1,0:T(1,128)S(1)} %bitcast.35, ...), custom_call_target="tpu_custom_call" | custom-call | tf_op jit(solution)/shard_map/second_image/pallas_call | solution.py:222
  103.0 1.5 collective-permute-start.1
  105.0 1.1 copy.50
  106.2 6.1 %scatter_custom_fusion = f32[3,4096]{0,1:T(8,128)S(1)} fusion(s32[2048]{0:T(1024)S(1)} %bitcast.45, f32[2048,3]{1,0:T(8,128)S(1)} %copy.50, f32[]{:T(128)} %constant.25.clone.1), kind=kCustom, calls=%fused_computation.2 | custom fusion | bytes 49156 | tf_op jit(solution)/shard_map/scatter | solution.py:242
  113.6 2.5 %collective-permute-start.9 = (f32[1,128]{1,0:T(1,128)S(1)}, f32[1,128]{1,0:T(1,128)S(1)}, u32[]{:S(2)}, u32[]{:S(2)}) collective-permute-start(f32[1,128]{1,0:T(1,128)S(1)} %add_add_fusion.1), channel_id=1, source_target_pairs={{0,7},{1,0},{2,1},{3,2},{4,3},{5,4},{6,5},{7,6},{8,15},{9,8},{10,9... | collective-permute-start | bytes 1544 | tf_op jit(solution)/shard_map/ppermute | solution.py:192
  120.2 2.5 %collective-permute-start.6 = (f32[1,128]{1,0:T(1,128)S(1)}, f32[1,128]{1,0:T(1,128)S(1)}, u32[]{:S(2)}, u32[]{:S(2)}) collective-permute-start(f32[1,128]{1,0:T(1,128)S(1)} %add_add_fusion.1), channel_id=1, source_target_pairs={{0,4},{1,5},{2,6},{3,7},{4,0},{5,1},{6,2},{7,3},{8,12},{9,13},{10,... | collective-permute-start | bytes 1544 | tf_op jit(solution)/shard_map/ppermute | solution.py:192
  123.3 1.5 collective-permute-start.4
  124.8 1.0 collective-permute-start.3
  127.2 12.3 %block_field.1 = f32[16,4096]{1,0:T(8,128)S(1)} custom-call(s32[8]{0:T(128)S(1)} %get-tuple-element.13.counts_ref, s32[8]{0:T(128)S(1)} %copy-done.4, f32[3,4096]{1,0:T(4,128)S(1)} %copy.51.points_ref, f32[6,8192]{1,0:T(8,128)S(1)} %all_gather.6.geo_ref, f32[2,8192]{1,0:T(2,128)S(1)} %get-tuple-element.7.basis_ref), custom_call_target="tpu_custom_call" | custom-call | tf_op jit(solution)/shard_map/block_field/pallas_call | solution.py:245
  146.5 5.5 %gather_fusion = f32[2048,6]{1,0:T(8,128)S(1)} fusion(f32[6,4096]{0,1:T(8,128)S(1)} %copy.52, s32[2048]{0:T(1024)S(1)} %copy-done.6), kind=kCustom, calls=%fused_computation | custom fusion | bytes 106496 | tf_op jit(solution)/shard_map/gather | solution.py:271
  (43 shorter events, 9.7 us)
Async XLA Ops:
  78.5 0.7 copy-start
  79.1 0.7 copy-start.2
  85.5 9.8 %all-to-all-start = ((f32[32,1,256]{2,1,0:T(1,128)}), f32[32,1,256]{2,1,0:T(1,128)S(1)}, u32[]{:S(2)}, u32[]{:S(2)}) async-start(f32[32,1,256]{2,1,0:T(1,128)} %broadcast_in_dim.23), calls=%async_computation | async-start | bytes 65536 | tf_op jit(solution)/shard_map/all_to_all | solution.py:221
  95.3 0.7 copy-start.1
  95.9 0.7 copy-start.3
  102.7 10.2 %collective-permute-start.2 = (f32[1,128]{1,0:T(1,128)}, f32[1,128]{1,0:T(1,128)}, u32[]{:S(2)}, u32[]{:S(2)}) collective-permute-start(f32[1,128]{1,0:T(1,128)} %slice.69), channel_id=1, source_target_pairs={{0,24},{8,0},{16,8},{24,16},{1,25},{9,1},{17,9},{25,17},{2,26},{10... | collective-permute-start | bytes 1544 | tf_op jit(solution)/shard_map/ppermute | solution.py:192
  103.0 10.0 %collective-permute-start.1 = (f32[1,128]{1,0:T(1,128)}, f32[1,128]{1,0:T(1,128)}, u32[]{:S(2)}, u32[]{:S(2)}) collective-permute-start(f32[1,128]{1,0:T(1,128)} %slice.69), channel_id=1, source_target_pairs={{0,16},{8,24},{16,0},{24,8},{1,17},{9,25},{17,1},{25,9},{2,18},{10... | collective-permute-start | bytes 1544 | tf_op jit(solution)/shard_map/ppermute | solution.py:192
  104.4 8.5 %collective-permute-start = (f32[1,128]{1,0:T(1,128)}, f32[1,128]{1,0:T(1,128)}, u32[]{:S(2)}, u32[]{:S(2)}) collective-permute-start(f32[1,128]{1,0:T(1,128)} %slice.69), channel_id=1, source_target_pairs={{0,8},{8,16},{16,24},{24,0},{1,9},{9,17},{17,25},{25,1},{2,10},{10... | collective-permute-start | bytes 1544 | tf_op jit(solution)/shard_map/ppermute | solution.py:192
  106.2 21.0 %copy-start.4 = (s32[8]{0:T(128)S(1)}, s32[8]{0:T(128)}, u32[]{:S(2)}) copy-start(s32[8]{0:T(128)} %length_ref.1) | copy-start | bytes 100
  112.9 33.6 %copy-start.6 = (s32[2048]{0:T(1024)S(1)}, s32[2048]{0:T(1024)}, u32[]{:S(2)}) copy-start(s32[2048]{0:T(1024)} %broadcast_clamp_fusion) | copy-start | bytes 24580
  113.6 9.7 %collective-permute-start.9 = (f32[1,128]{1,0:T(1,128)S(1)}, f32[1,128]{1,0:T(1,128)S(1)}, u32[]{:S(2)}, u32[]{:S(2)}) collective-permute-start(f32[1,128]{1,0:T(1,128)S(1)} %add_add_fusion.1), channel_id=1, source_target_pairs={{0,7},{1,0},{2,1},{3,2},{4,3},{5,4},{6,5},{7,6},{8,15},{9,8},{10,9... | collective-permute-start | bytes 1544 | tf_op jit(solution)/shard_map/ppermute | solution.py:192
  116.1 8.7 %collective-permute-start.8 = (f32[1,128]{1,0:T(1,128)S(1)}, f32[1,128]{1,0:T(1,128)S(1)}, u32[]{:S(2)}, u32[]{:S(2)}) collective-permute-start(f32[1,128]{1,0:T(1,128)S(1)} %add_add_fusion.1), channel_id=1, source_target_pairs={{0,6},{1,7},{2,0},{3,1},{4,2},{5,3},{6,4},{7,5},{8,14},{9,15},{10,... | collective-permute-start | bytes 1544 | tf_op jit(solution)/shard_map/ppermute | solution.py:192
  119.8 19.7 %collective-permute-start.7 = (f32[1,128]{1,0:T(1,128)S(1)}, f32[1,128]{1,0:T(1,128)S(1)}, u32[]{:S(2)}, u32[]{:S(2)}) collective-permute-start(f32[1,128]{1,0:T(1,128)S(1)} %add_add_fusion.1), channel_id=1, source_target_pairs={{0,5},{1,6},{2,7},{3,0},{4,1},{5,2},{6,3},{7,4},{8,13},{9,14},{10,... | collective-permute-start | bytes 1544 | tf_op jit(solution)/shard_map/ppermute | solution.py:192
  120.2 19.3 %collective-permute-start.6 = (f32[1,128]{1,0:T(1,128)S(1)}, f32[1,128]{1,0:T(1,128)S(1)}, u32[]{:S(2)}, u32[]{:S(2)}) collective-permute-start(f32[1,128]{1,0:T(1,128)S(1)} %add_add_fusion.1), channel_id=1, source_target_pairs={{0,4},{1,5},{2,6},{3,7},{4,0},{5,1},{6,2},{7,3},{8,12},{9,13},{10,... | collective-permute-start | bytes 1544 | tf_op jit(solution)/shard_map/ppermute | solution.py:192
  122.8 16.7 %collective-permute-start.5 = (f32[1,128]{1,0:T(1,128)S(1)}, f32[1,128]{1,0:T(1,128)S(1)}, u32[]{:S(2)}, u32[]{:S(2)}) collective-permute-start(f32[1,128]{1,0:T(1,128)S(1)} %add_add_fusion.1), channel_id=1, source_target_pairs={{0,3},{1,4},{2,5},{3,6},{4,7},{5,0},{6,1},{7,2},{8,11},{9,12},{10,... | collective-permute-start | bytes 1544 | tf_op jit(solution)/shard_map/ppermute | solution.py:192
  123.3 16.2 %collective-permute-start.4 = (f32[1,128]{1,0:T(1,128)S(1)}, f32[1,128]{1,0:T(1,128)S(1)}, u32[]{:S(2)}, u32[]{:S(2)}) collective-permute-start(f32[1,128]{1,0:T(1,128)S(1)} %add_add_fusion.1), channel_id=1, source_target_pairs={{0,2},{1,3},{2,4},{3,5},{4,6},{5,7},{6,0},{7,1},{8,10},{9,11},{10,... | collective-permute-start | bytes 1544 | tf_op jit(solution)/shard_map/ppermute | solution.py:192
  124.8 14.7 %collective-permute-start.3 = (f32[1,128]{1,0:T(1,128)S(1)}, f32[1,128]{1,0:T(1,128)S(1)}, u32[]{:S(2)}, u32[]{:S(2)}) collective-permute-start(f32[1,128]{1,0:T(1,128)S(1)} %add_add_fusion.1), channel_id=1, source_target_pairs={{0,1},{1,2},{2,3},{3,4},{4,5},{5,6},{6,7},{7,0},{8,9},{9,10},{10,1... | collective-permute-start | bytes 1544 | tf_op jit(solution)/shard_map/ppermute | solution.py:192
  145.9 6.5 %copy-start.5 = (f32[3,2048]{1,0:T(4,128)S(1)}, f32[3,2048]{1,0:T(4,128)}, u32[]{:S(2)}) copy-start(f32[3,2048]{1,0:T(4,128)} %param.11) | copy-start | bytes 73732
